TPU v7x, 256 devices: a whole 4x4x8 slice. The times are simulated.
256 devices in a mesh: row: 64 (over z, x, core), ba: 4 (over y).
Axes of the slice: x: 4, y: 4, z: 8, core: 2. Of those that a mesh axis runs over, the one named last changes fastest.
Arguments:
- constants: float32 [64, 192, 36864], P('row', 'ba'), may hold values from -6 to 6
- current_modes: float32 [64, 2, 192, 4], P('row', None, 'ba'), may hold values from -0.4375 to 0.4375
- owner_id: int32 [1], replicated, may hold values from 0 to 63
- live_count: int32 [64], P('row'), may hold values from 0 to 1, as said below
- triplets: int32 [64, 6], P('row'), may hold values from -3 to 3
- center_point: int32 [3], replicated, may hold values from 0 to 31
- pair_points: int32 [512, 3], P('row'), may hold values from 0 to 31
- first_vectors: float32 [512, 2, 36864], P('row'), may hold values from -0.4375 to 0.4375
- second_vectors: float32 [512, 2, 36864], P('row'), may hold values from -0.4375 to 0.4375
Outputs:
- strength: float32 [512, 4, 36864], P('row', 'ba')
Inputs may be any that keep to these rules, and one draw needn't show every extreme that they name: Shard j uses its first live_count[j] slots; the constants and triplets of the other slots are ignored. A shard may use none. Some shard uses all 1 slots.
All inputs are finite; a program needn't handle non-finite values.
Results may differ from a plain program's by a relative error of at most 0.00008.
Values sent between devices are 32-bit elements; how exact they have to be, the bound alone decides.
A program may use at most 128 MiB of HBM per device.

v0:
```python
import math

import jax
import jax.numpy as jnp
from jax import lax
from jax.sharding import PartitionSpec as P

B = 192
G = 32


HIGHEST = lax.Precision.HIGHEST
FULL_TURN = 2.0 * math.pi


def broadcast(shard, axis, root):
    mine = lax.axis_index(axis) == root
    return lax.psum(jnp.where(mine, shard, jnp.zeros_like(shard)), axis)


def rotation_table(pair_rows, shift_rows, grid_size):
    turns = (
        jnp.sum(pair_rows[:, :, None] * shift_rows[None, 0:3, :], axis=1) - shift_rows[3][None, :]
    )
    angle = jnp.mod(turns, grid_size).astype(jnp.float32) * (FULL_TURN / grid_size)
    cosine = jnp.cos(angle)
    sine = jnp.sin(angle)
    upper_row = jnp.stack([cosine, -sine], axis=1)
    lower_row = jnp.stack([sine, cosine], axis=1)
    return jnp.stack([upper_row, lower_row], axis=1)


def complex_block(vectors, branches):
    pair_count = vectors.shape[0]
    real_part = vectors[:, 0].reshape(pair_count, branches, branches)
    imag_part = vectors[:, 1].reshape(pair_count, branches, branches)
    upper_row = jnp.stack([real_part, -imag_part], axis=1)
    lower_row = jnp.stack([imag_part, real_part], axis=1)
    return jnp.stack([upper_row, lower_row], axis=1)


def strengths(phase_sum, first_vectors, second_vectors, branches, total_slots):
    pair_count = phase_sum.shape[0]
    band_count = phase_sum.shape[1]
    shaped = phase_sum.reshape(pair_count, band_count, 2, branches, branches)
    partial_sum = jnp.einsum(
        "knibc,koicm->knobm", shaped, complex_block(second_vectors, branches), precision=HIGHEST
    )
    amplitude = jnp.einsum(
        "kojbp,knjbm->knopm", complex_block(first_vectors, branches), partial_sum, precision=HIGHEST
    )
    result = (
        amplitude[:, :, 0] * amplitude[:, :, 0] + amplitude[:, :, 1] * amplitude[:, :, 1]
    ) / total_slots
    return result.reshape(pair_count, band_count, branches * branches)


def body(
    constants,
    current_modes,
    owner_id,
    live_count,
    triplets,
    center_point,
    pair_points,
    first_vectors,
    second_vectors,
):
    slot_count = constants.shape[0]
    eigen = broadcast(current_modes[0], "row", owner_id[0])
    weight = (jnp.arange(slot_count, dtype=jnp.int32) < live_count[0]).astype(jnp.float32)
    term = jnp.einsum("san,rax->nsrx", eigen, constants, precision=HIGHEST)
    contracted = lax.psum_scatter(
        term * weight[None, None, :, None], "ba", scatter_dimension=0, tiled=True
    )
    second_cell = triplets[:, 3:6]
    offsets = triplets[:, 0:3] - second_cell
    point_shift = jnp.sum(second_cell * center_point[None, :], axis=1)
    shift_rows = jnp.concatenate([offsets.T, point_shift[None, :]], axis=0)
    geometry = shift_rows.astype(jnp.float32)[None]
    shard_block = lax.all_gather(contracted, "row", axis=2, tiled=True)
    shard_geometry = lax.all_gather(geometry, "row", axis=2, tiled=True)
    rotation = rotation_table(pair_points, shard_geometry[0].astype(jnp.int32), G)
    phase_sum = jnp.einsum("kuir,nirx->knux", rotation, shard_block, precision=HIGHEST)
    total_slots = slot_count * lax.axis_size("row")
    return strengths(phase_sum, first_vectors, second_vectors, B, total_slots)


def solution(mesh):
    return jax.shard_map(
        body,
        mesh=mesh,
        in_specs=(
            P("row", "ba", None),
            P("row", None, "ba", None),
            P(),
            P("row"),
            P("row", None),
            P(),
            P("row", None),
            P("row", None, None),
            P("row", None, None),
        ),
        out_specs=P("row", "ba", None),
        check_vma=False,
    )
```

profile of v0, /device:TPU:1, one launch (start us, length us, event | category | flops | bytes accessed | tf_op | source)
XLA Modules:
  0.0 357.4 jit_solution(16064091335156367080)
XLA Ops:
  7.9 128.0 %psum.7 = f32[2,48,4]{1,2,0:T(4,128)S(1)} all-reduce(f32[2,48,4]{1,2,0:T(4,128)S(1)} %select_bitcast_fusion), channel_id=1, replica_groups=mesh['row'=64,'ba'=4] {'row'}, use_global_device_ids=true, to_apply=%region_0.1 | all-reduce | flops 384 | bytes 3072 | tf_op jit(solution)/shard_map/psum | solution.py:18
  135.9 5.8 %fusion = f32[4,2,1,36864]{3,0,1,2:T(4,128)S(1)} fusion(f32[2,48,4]{1,2,0:T(4,128)S(1)} %psum.7, f32[1,48,36864]{2,1,0:T(8,128)} %param.9, f32[]{:T(128)} %bitcast.6), kind=kOutput, calls=%fused_computation.2 | convolution fusion | flops 170164224 | bytes 8259076 | tf_op jit(solution)/shard_map/san,rax->nsrx/dot_general | solution.py:72
  141.7 1.9 copy.51
  143.7 0.6 dynamic-slice
  144.4 49.2 %all-reduce.3.cloned.1.call-done = f32[4,2,1,36864]{3,1,2,0:T(2,128)} async-done(((f32[4,2,1,36864]{3,1,2,0:T(2,128)}), f32[4,2,1,36864]{3,1,2,0:T(2,128)}) %all-reduce.3.cloned.1.call-update) | async-done | bytes 1179664
  193.6 2.3 dynamic-slice_bitcast_fusion
  195.9 0.7 subtract_bitcast_fusion
  196.7 0.7 fusion.29
  197.4 43.0 %all_gather.7 = f32[1,4,64]{1,0,2:T(1,128)S(1)} all-gather(f32[1,4,1]{1,0,2:T(1,128)S(1)} %fusion.29), channel_id=1, replica_groups=mesh['row'=64,'ba'=4] {'row'}, dimensions={2}, use_global_device_ids=true | all-gather | bytes 1040 | tf_op jit(solution)/shard_map/all_gather | solution.py:82
  240.5 9.8 %slice_reduce_fusion = (f32[8,36864]{1,0:T(8,128)}, f32[8,36864]{1,0:T(8,128)S(1)}) fusion(f32[8,2,36864]{2,1,0:T(2,128)} %param.16), kind=kLoop, calls=%fused_computation.25 | loop fusion | bytes 4718592 | tf_op jit(solution)/shard_map/slice | solution.py:36
  250.3 2.0 reshape_squeeze.7
  252.3 2.0 stack_reshape_squeeze.5
  254.3 10.4 %slice_reduce_fusion.2 = (f32[8,36864]{1,0:T(8,128)S(1)}, f32[8,36864]{1,0:T(8,128)}) fusion(f32[8,2,36864]{2,1,0:T(2,128)} %param.17), kind=kLoop, calls=%fused_computation.27 | loop fusion | bytes 4718592 | tf_op jit(solution)/shard_map/slice | solution.py:36
  264.7 1.9 reshape_squeeze.6
  266.6 2.0 copy.47
  268.6 1.3 neg.30
  269.9 3.2 stack_reshape_squeeze.4
  273.1 3.2 copy.48
  276.3 0.1 multiply_reduce_fusion
  276.4 1.3 slice_reduce_fusion.4
  277.8 6.1 %maximum_bitcast_fusion = (f32[8,1,2,192,192]{3,4,2,1,0:T(8,128)}, f32[8,1,2,192,192]{3,4,2,1,0:T(8,128)}) fusion(f32[8,1,192,192]{2,3,1,0:T(8,128)} %neg.30, f32[8,1,192,192]{2,3,1,0:T(8,128)} %copy.48, f32[8,1,192,192]{2,3,1,0:T(8,128)S(1)} %copy.47), kind=kLoop, calls=%fused_computation.14 | loop fusion | flops 1179648 | bytes 8257536 | tf_op jit(solution)/shard_map/stack | solution.py:39
  283.8 0.1 bitcast_negate_fusion
  284.0 1.3 copy-done.2
  285.3 3.6 %maximum_bitcast_fusion.2 = (f32[8,1,2,192,192]{4,3,2,1,0:T(8,128)}, f32[8,1,2,192,192]{4,3,2,1,0:T(8,128)}) fusion(f32[8,1,192,192]{3,2,1,0:T(8,128)S(1)} %bitcast_negate_fusion, f32[8,1,192,192]{3,2,1,0:T(8,128)S(1)} %bitcast.102, f32[8,1,192,192]{3,2,1,0:T(8,128)S(1)} %bitcast.101), kind=kLoop, calls=%fused_computation.16 | loop fusion | flops 1179648 | bytes 8257536 | tf_op jit(solution)/shard_map/stack | solution.py:39
  288.9 14.8 %all-gather.2.cloned.1.call-done = f32[1,2,64,36864]{3,1,0,2:T(2,128)} async-done(((f32[1,2,1,36864]{3,1,0,2:T(2,128)}), f32[1,2,64,36864]{3,1,0,2:T(2,128)}) %all-gather.2.cloned.1.call-update) | async-done | bytes 18874384 | tf_op jit(solution)/shard_map/all_gather | solution.py:81
  303.8 26.1 %convolution_bitcast_fusion = f32[8,1,2,36864]{3,0,2,1:T(8,128)} fusion(f32[1,2,64,36864]{3,1,0,2:T(2,128)} %all-gather.2.cloned.1.call-done, f32[8,1,2,64]{3,0,2,1:T(8,128)S(1)} %get-tuple-element.17, f32[8,1,2,64]{3,0,2,1:T(8,128)S(1)} %get-tuple-element.16), kind=kOutput, calls=%fused_computation | convolution fusion | flops 905971712 | bytes 21241856 | tf_op jit(solution)/shard_map/kuir,nirx->knux/dot_general | solution.py:84
  329.8 2.7 reshape.272
  332.6 8.3 %fusion.4 = f32[8,2,192,192,1]{3,2,4,1,0:T(8,128)S(1)} fusion(f32[8,1,2,192,192]{3,4,2,1,0:T(8,128)} %get-tuple-element.12, f32[8,1,2,192,192]{3,4,2,1,0:T(8,128)} %get-tuple-element.11, f32[8,2,192,192]{3,2,0,1:T(8,128)S(1)} %reshape.272), kind=kOutput, calls=%fused_computation.6 | convolution fusion | flops 2719088640 | bytes 9437184 | tf_op jit(solution)/shard_map/knibc,koicm->knobm/dot_general | solution.py:46
  340.9 6.0 %fusion.14 = f32[8,1,2,192,192]{3,4,2,0,1:T(8,128)S(1)} fusion(f32[8,1,2,192,192]{4,3,2,1,0:T(8,128)S(1)} %copy-done.1, f32[8,1,2,192,192]{4,3,2,1,0:T(8,128)S(1)} %copy-done, f32[8,2,192,192,1]{3,2,4,1,0:T(8,128)S(1)} %fusion.4), kind=kOutput, calls=%fused_computation.20 | convolution fusion | flops 2719088640 | bytes 9437184 | tf_op jit(solution)/shard_map/kojbp,knjbm->knopm/dot_general | solution.py:49
  347.0 0.2 fusion.20
  347.2 0.6 copy.61
  347.8 2.5 div.11
  (22 shorter events, 0.3 us)
Async XLA Ops:
  6.5 187.1 %all-reduce.3.cloned.1.call-start = ((), (), s32[]{:S(2)}) async-start(), calls=%async_computation.1 | async-start | bytes 2359296
  141.7 2.0 copy-start.6
  141.7 54.2 %copy-start.3 = (s32[1,6]{1,0:T(1,128)S(1)}, s32[1,6]{1,0:T(1,128)}, u32[]{:S(2)}) copy-start(s32[1,6]{1,0:T(1,128)} %param.13) | copy-start | bytes 76
  141.7 54.2 %copy-start.5 = (s32[3]{0:T(128)S(1)}, s32[3]{0:T(128)}, u32[]{:S(2)}) copy-start(s32[3]{0:T(128)} %param.14) | copy-start | bytes 40
  143.7 160.1 %all-gather.2.cloned.1.call-start = ((), (), s32[]{:S(2)}) async-start(), calls=%async_computation | async-start | bytes 19169280 | tf_op jit(solution)/shard_map/all_gather | solution.py:81
  269.9 6.4 %copy-start.4 = (s32[8,3]{0,1:T(4,128)S(1)}, s32[8,3]{0,1:T(4,128)}, u32[]{:S(2)}) copy-start(s32[8,3]{0,1:T(4,128)} %param.15) | copy-start | bytes 292
  283.8 1.4 copy-start.2
  332.6 8.4 %copy-start = (f32[8,1,2,192,192]{4,3,2,1,0:T(8,128)S(1)}, f32[8,1,2,192,192]{4,3,2,1,0:T(8,128)}, u32[]{:S(2)}) copy-start(f32[8,1,2,192,192]{4,3,2,1,0:T(8,128)} %get-tuple-element.13) | copy-start | bytes 7077892
  332.6 8.4 %copy-start.1 = (f32[8,1,2,192,192]{4,3,2,1,0:T(8,128)S(1)}, f32[8,1,2,192,192]{4,3,2,1,0:T(8,128)}, u32[]{:S(2)}) copy-start(f32[8,1,2,192,192]{4,3,2,1,0:T(8,128)} %get-tuple-element.14) | copy-start | bytes 7077892
Sparse Core Ops, SparseCore 0:
  143.8 49.7 all-reduce.2
  196.3 107.3 all-gather.1
where the time goes:
time: 361 us; the launch traced here: 357 us
  blocking collectives  171 us (47%)
  waiting for transfers between devices  64.1 us (18%)
  local copies, waits for them, and re-layouts  47.9 us (13%)
  matrix products  46.2 us (13%)
  between operations  15.1 us (4%)
  other arithmetic  12.9 us (4%)
    psum x1, blocking collectives, broadcast(): return lax.psum(jnp.where(mine, shard, jnp.zeros_like(shard)), axis)  128 us
    unnamed x3, waiting for transfers between devices  49.3 us
    all_gather x1, blocking collectives, body(): shard_geometry = lax.all_gather(geometry, 'row', axis=2, tiled=True)  43 us
    dot_general x1, matrix products, body(): jnp.einsum('kuir,nirx->knux', rotation, shard_block, precision=HIGHEST)  26.1 us
    slice x2, local copies, waits for them, and re-layouts, complex_block(): imag_part = vectors[:, 1].reshape(pair_count, branches, branches)  20.2 us
    all_gather x1, waiting for transfers between devices, body(): shard_block = lax.all_gather(contracted, 'row', axis=2, tiled=True)  14.8 us
    another operation x2, other arithmetic, complex_block(): return jnp.stack([upper_row, lower_row], axis=1)  9.72 us
    another operation x3, local copies, waits for them, and re-layouts, complex_block(): upper_row = jnp.stack([real_part, -imag_part], axis=1)  8.34 us
  transfers between devices with their start and end apart: 2, of which 2 were waited for; matrix products, arithmetic and copies ran while one was open for 14% of the time, Pallas kernels for 0%

commit v1 on v0

v1 whole, which is shorter than its diff:
```python
import functools
import math

import jax
import jax.numpy as jnp
from jax import lax
from jax.experimental import pallas as pl
from jax.experimental.pallas import tpu as pltpu
from jax.sharding import PartitionSpec as P

B = 192
G = 32
Z, X = 8, 4
Q = 2 * X
R = Z * Q
LANES = 128
TILES = B * B // LANES
SHARE = TILES // Q
J = 3
TT = SHARE // J
BLK = 2 * TT
HALF = Q // 2
PAIRS = 8
KO = 2 * PAIRS
MESH = pl.DeviceIdType.MESH
F32 = jnp.float32
BF16 = jnp.bfloat16


def split(value):
    high = value.astype(BF16)
    return high, (value - high.astype(F32)).astype(BF16)


def dot(a, b):
    return lax.dot_general(a, b, (((1,), (0,)), ((), ())), preferred_element_type=F32)


def dot3(ah, al, bh, bl):
    return dot(ah, bh) + dot(al, bh) + dot(ah, bl)


def kernel(
    sum_ref, points_ref, live_ref, const_ref, first_ref, second_ref, out_ref,
    const_v, first_v, second_v, got1, got2, rot, lhs, term, part1, part2, final,
    gathered, phase_out, phase_in, square, first_t, second_m,
    const_sem, vec_sem, s1, r1, s2, r2, sy1, ry1, sy2, ry2, sc, rc, sz, rz, sp, rp,
):
    row = lax.axis_index("row")
    y = lax.axis_index("ba")
    z = row // Q
    q = row % Q
    x = q // 2
    core = q % 2
    ya = y + 1 - 2 * (y % 2)
    yb = 3 - y
    y2 = (y + 2) % 4

    def qpeer(i):
        return ((x + i // 2) % X) * 2 + (core + i % 2) % 2

    def zpeer(i):
        return (z + i) % Z

    const_copies = {}
    for j in range(J):
        for p in range(Q):
            copy = pltpu.make_async_copy(
                const_ref.at[:, pl.ds((p * SHARE + j * TT) * LANES, TT * LANES)],
                const_v.at[j, p],
                const_sem.at[j, p],
            )
            copy.start()
            const_copies[j, p] = copy
    second_copy = pltpu.make_async_copy(second_ref, second_v, vec_sem.at[0])
    second_copy.start()
    first_copy = pltpu.make_async_copy(first_ref, first_v, vec_sem.at[1])
    first_copy.start()

    barrier = pltpu.get_barrier_semaphore()
    for i in range(1, Z):
        pl.semaphore_signal(barrier, inc=1, device_id=(zpeer(i) * Q + q, y), device_id_type=MESH)
    for i in range(1, Q):
        pl.semaphore_signal(barrier, inc=1, device_id=(z * Q + qpeer(i), y), device_id_type=MESH)
    for other in (ya, yb):
        pl.semaphore_signal(barrier, inc=1, device_id=(row, other), device_id_type=MESH)
    pl.semaphore_wait(barrier, Z - 1 + Q - 1 + 2)

    def remote(src, dst, send, recv, device):
        return pltpu.make_async_remote_copy(
            src_ref=src, dst_ref=dst, send_sem=send, recv_sem=recv,
            device_id=device, device_id_type=MESH,
        )

    copies1 = []
    for i in range(1, Z):
        copy = remote(sum_ref, got1.at[i], s1.at[i], r1.at[i], (zpeer(i) * Q + q, y))
        copy.start()
        copies1.append(copy)
    for copy in copies1:
        copy.wait_recv()
    total = sum_ref[...]
    for i in range(1, Z):
        total = total + got1[i]
    got2[q, 0:16] = total
    got2[q, 16:32] = points_ref[...]
    copies2 = []
    for i in range(1, Q):
        copy = remote(got2.at[q], got2.at[q], s2.at[i], r2.at[i], (z * Q + qpeer(i), y))
        copy.start()
        copies2.append(copy)

    def paired(ref, k, start, stride):
        tiles = [ref[k, pl.ds(start + stride // 3 * i, B // 2, stride=stride), :] for i in range(3)]
        even = jnp.concatenate(tiles[0:2], axis=1)
        odd = pltpu.roll(jnp.concatenate(tiles[1:3], axis=1), 192, 1)
        return even, odd

    def prepare_second(k, carry):
        for o in range(2):
            even, odd = paired(second_v, k, o, 6)
            for i in range(2):
                lanes = slice(i * LANES, (i + 1) * LANES)
                square[i, pl.ds(0, B // 2, stride=2), :] = even[:, lanes]
                square[i, pl.ds(1, B // 2, stride=2), :] = odd[:, lanes]
            high, low = split(jnp.concatenate([square[0, 0:B, :], square[1, 0:B, :]], axis=1))
            zero = jnp.zeros((256 - B, 256), BF16)
            second_m[k, o, 0] = jnp.concatenate([high, zero], axis=0)
            second_m[k, o, 1] = jnp.concatenate([low, zero], axis=0)
        return carry

    def prepare_first(k, carry):
        for o in range(2):
            even, odd = paired(first_v, k, o, 6)
            zero = jnp.zeros((256 - B, 256), F32)
            turned = jnp.transpose(jnp.concatenate([even, odd, zero], axis=0))
            for i in range(2):
                lanes = slice(i * LANES, (i + 1) * LANES)
                square[i] = turned[:, lanes]
                for parity in range(2):
                    high, low = split(square[i, pl.ds(parity, B // 2, stride=2), :])
                    rows = slice(parity * (B // 2), (parity + 1) * (B // 2))
                    first_t[k, o, 0, rows, lanes] = high
                    first_t[k, o, 1, rows, lanes] = low
        return carry

    second_copy.wait()
    lax.fori_loop(0, PAIRS, prepare_second, 0)

    for copy in copies2:
        copy.wait_recv()
    total = got2[0, 0:16]
    for i in range(1, Q):
        total = total + got2[i, 0:16]
    points = jnp.concatenate([got2[i, 16:32] for i in range(Q)], axis=0)
    turns = -total[11:12]
    for axis in range(3):
        turns = turns + points[:, axis : axis + 1] * total[8 + axis : 9 + axis]
    lane = lax.broadcasted_iota(jnp.int32, (Q * KO, LANES), 1)
    line = lax.broadcasted_iota(jnp.int32, (Q * KO, LANES), 0)
    turns = turns + jnp.where(lane >= R, 8.0, 0.0) - jnp.where(line % 2 == 1, 8.0, 0.0)
    turns = turns - G * jnp.floor(turns * (1.0 / G))
    high, low = split(jnp.cos(turns * (2.0 * math.pi / G)))
    rot[:, 0:128] = high
    rot[:, 128:256] = low
    eigen = total[0:8] * jnp.where(live_ref[0] > 0, 1.0, 0.0)
    high, low = split(eigen)
    lane8 = lax.broadcasted_iota(jnp.int32, (8, LANES), 1)
    lhs[...] = jnp.concatenate(
        [high.astype(F32), jnp.where(lane8 < 48, low.astype(F32), 0.0)], axis=0
    ).astype(BF16)

    def contract(j):
        def step(p, carry):
            pltpu.make_async_copy(const_ref.at[:, pl.ds(0, TT * LANES)], const_v.at[j, p], const_sem.at[j, p]).wait()
            high, low = split(const_v[j, p])
            both = dot(lhs[:, 0:96], jnp.concatenate([high, low], axis=0))
            both = both[0:8] + both[8:16]
            for t in range(TT):
                term[j, p, pl.ds(t, 8, stride=TT), :] = both[:, t * LANES : (t + 1) * LANES]
            return carry

        lax.fori_loop(0, Q, step, 0)

    waits = []

    def go(copy):
        copy.start()
        waits.append(copy)
        return copy

    def band(j, h, n):
        return term.at[j, pl.ds(HALF * h, HALF), pl.ds(pl.multiple_of(n * BLK, 8), BLK), :]

    y1, yy2, c2a, ring, p2a = {}, {}, {}, {}, {}

    def y1_start(j):
        for h, other in enumerate((ya, yb)):
            for slot, n in enumerate((other, y2)):
                y1[j, h, slot] = go(remote(
                    band(j, h, n), part1.at[j, h, slot], sy1.at[j, h, slot], ry1.at[j, h, slot], (row, other)
                ))

    def y2_start(j):
        for h, other in enumerate((yb, ya)):
            y1[j, h, 1].wait_recv()
            mine = band(j, h, other)
            mine[...] = mine[...] + part1[j, h, 1]
            yy2[j, h] = go(remote(mine, part2.at[j, h], sy2.at[j, h], ry2.at[j, h], (row, other)))

    def slot_rows(r, count=1):
        return pl.ds(pl.multiple_of(r * BLK, 8), count * BLK)

    def c2a_start(j):
        for h in range(2):
            y1[j, h, 0].wait_recv()
            yy2[j, h].wait_recv()
            final[j, HALF * h : HALF * (h + 1)] = band(j, h, y)[...] + part1[j, h, 0] + part2[j, h]
        gathered[j, slot_rows(row), :] = final[j, q]
        for i in range(1, Q):
            c2a[j, i] = go(remote(
                final.at[j, qpeer(i)], gathered.at[j, slot_rows(row), :], sc.at[j, i], rc.at[j, i],
                (z * Q + qpeer(i), y),
            ))

    def ring_start(j, i):
        if i == 1:
            for n in range(1, Q):
                c2a[j, n].wait_recv()
        else:
            for side in range(2):
                ring[j, i - 1, side].wait_recv()
        for side, sign in enumerate((1, -1)):
            base = ((z + Z - sign * (i - 1)) % Z) * Q
            rows = slot_rows(base, Q) if i < 4 else slot_rows(base + HALF * side, HALF)
            block = gathered.at[j, rows, :]
            ring[j, i, side] = go(remote(
                block, block, sz.at[j, i, side], rz.at[j, i, side], (((z + Z + sign) % Z) * Q + q, y)
            ))

    def phase(j):
        for side in range(2):
            ring[j, 4, side].wait_recv()

        def step(u, carry):
            cols = []
            for v in range(2):
                t = 2 * u + v
                cols.append(jnp.concatenate(
                    [gathered[j, pl.ds(s * TT + t, R, stride=BLK), :] for s in range(2)], axis=0
                ))
            high, low = split(jnp.concatenate(cols, axis=1))
            value = dot(rot[...], jnp.concatenate([high, high], axis=0)) + dot(rot[:, 0:128], low)
            for v in range(2):
                for d in range(Q):
                    phase_out[j, d, pl.ds(pl.multiple_of((2 * u + v) * KO, 8), KO), :] = value[
                        d * KO : (d + 1) * KO, v * LANES : (v + 1) * LANES
                    ]
            return carry

        lax.fori_loop(0, TT // 2, step, 0)
        rows = pl.ds(pl.multiple_of((q * SHARE + j * TT) * KO, 8), TT * KO)
        for i in range(1, Q):
            p2a[j, i] = go(remote(
                phase_out.at[j, qpeer(i)], phase_in.at[rows, :], sp.at[j, i], rp.at[j, i], (z * Q + qpeer(i), y)
            ))
        phase_in[rows, :] = phase_out[j, q]

    for j in range(J):
        contract(j)
        y1_start(j)
    for j in range(J):
        y2_start(j)
    for j in range(J):
        c2a_start(j)
    for j in range(J):
        ring_start(j, 1)
    first_copy.wait()
    lax.fori_loop(0, PAIRS, prepare_first, 0)
    for i in range(2, 5):
        for j in range(J):
            ring_start(j, i)
    for j in range(J):
        phase(j)
    for j in range(J):
        for i in range(1, Q):
            p2a[j, i].wait_recv()

    def finish(k, carry):
        planes = []
        for o in range(2):
            tiles = [
                phase_in[pl.ds(KO * i + 2 * k + o, B // 2, stride=3 * KO), :] for i in range(3)
            ]
            even = jnp.concatenate(tiles[0:2], axis=1)
            odd = pltpu.roll(jnp.concatenate(tiles[1:3], axis=1), 192, 1)
            planes.append(split(jnp.concatenate([even, odd], axis=0)))
        (prh, prl), (pih, pil) = planes
        wr = (second_m[k, 0, 0], second_m[k, 0, 1])
        wi = (second_m[k, 1, 0], second_m[k, 1, 1])
        real = dot3(prh, prl, *wr) - dot3(pih, pil, *wi)
        imag = dot3(prh, prl, *wi) + dot3(pih, pil, *wr)
        zero = jnp.zeros((256 - B, 256), F32)
        tr = split(jnp.concatenate([real, zero], axis=0))
        ti = split(jnp.concatenate([imag, zero], axis=0))
        vr = (first_t[k, 0, 0], first_t[k, 0, 1])
        vi = (first_t[k, 1, 0], first_t[k, 1, 1])
        real = dot3(*vr, *tr) - dot3(*vi, *ti)
        imag = dot3(*vr, *ti) + dot3(*vi, *tr)
        value = (real * real + imag * imag) * (1.0 / R)
        even = value[0 : B // 2]
        odd = pltpu.roll(value[B // 2 : B], 64, 1)
        lane = lax.broadcasted_iota(jnp.int32, (B // 2, LANES), 1)
        out_ref[k, pl.ds(0, B // 2, stride=3), :] = even[:, 0:LANES]
        out_ref[k, pl.ds(1, B // 2, stride=3), :] = jnp.where(
            lane < 64, even[:, LANES:], odd[:, 0:LANES]
        )
        out_ref[k, pl.ds(2, B // 2, stride=3), :] = odd[:, LANES:]
        return carry

    lax.fori_loop(0, PAIRS, finish, 0)
    for copy in copies1 + copies2 + waits:
        copy.wait_send()


def linear(vectors):
    tiles = vectors.reshape(PAIRS, 2, TILES, LANES)
    return tiles.transpose(0, 2, 1, 3).reshape(PAIRS, 2 * TILES, LANES)


def body(
    constants,
    current_modes,
    owner_id,
    live_count,
    triplets,
    center_point,
    pair_points,
    first_vectors,
    second_vectors,
):
    row = lax.axis_index("row")
    eigen = jnp.where(row == owner_id[0], current_modes[0], 0.0)
    eigen = eigen.transpose(2, 0, 1).reshape(8, 48)
    eigen = jnp.concatenate([eigen, eigen, jnp.zeros((8, LANES - 96), F32)], axis=1)
    second_cell = triplets[0, 3:6]
    offsets = triplets[0, 0:3] - second_cell
    shift = jnp.sum(second_cell * center_point)
    geometry = jnp.concatenate([offsets, shift[None], jnp.zeros((4,), jnp.int32)]).astype(F32)
    lane = jnp.arange(LANES, dtype=jnp.int32)
    geometry = jnp.where((lane % R == row)[None, :], geometry[:, None], 0.0)
    sums = jnp.concatenate([eigen, geometry], axis=0)
    points = jnp.pad(jnp.repeat(pair_points.astype(F32), 2, axis=0), ((0, 0), (0, LANES - 3)))

    vmem = pl.BlockSpec(memory_space=pltpu.VMEM)
    anywhere = pl.BlockSpec(memory_space=pl.ANY)
    dma = pltpu.SemaphoreType.DMA
    out = pl.pallas_call(
        kernel,
        out_shape=jax.ShapeDtypeStruct((PAIRS, TILES, LANES), F32),
        in_specs=[vmem, vmem, pl.BlockSpec(memory_space=pltpu.SMEM), anywhere, anywhere, anywhere],
        out_specs=vmem,
        scratch_shapes=[
            pltpu.VMEM((J, Q, 48, TT * LANES), F32),
            pltpu.VMEM((PAIRS, 2 * TILES, LANES), F32),
            pltpu.VMEM((PAIRS, 2 * TILES, LANES), F32),
            pltpu.VMEM((Z, 16, LANES), F32),
            pltpu.VMEM((Q, 32, LANES), F32),
            pltpu.VMEM((Q * KO, 256), BF16),
            pltpu.VMEM((16, LANES), BF16),
            pltpu.VMEM((J, Q, 4 * BLK, LANES), F32),
            pltpu.VMEM((J, 2, 2, HALF, BLK, LANES), F32),
            pltpu.VMEM((J, 2, HALF, BLK, LANES), F32),
            pltpu.VMEM((J, Q, BLK, LANES), F32),
            pltpu.VMEM((J, R * BLK, LANES), F32),
            pltpu.VMEM((J, Q, TT * KO, LANES), F32),
            pltpu.VMEM((TILES * KO, LANES), F32),
            pltpu.VMEM((2, 256, LANES), F32),
            pltpu.VMEM((PAIRS, 2, 2, B, 256), BF16),
            pltpu.VMEM((PAIRS, 2, 2, 256, 256), BF16),
            dma((J, Q)), dma((2,)),
            dma((Z,)), dma((Z,)), dma((Q,)), dma((Q,)),
            dma((J, 2, 2)), dma((J, 2, 2)), dma((J, 2)), dma((J, 2)),
            dma((J, Q)), dma((J, Q)), dma((J, 5, 2)), dma((J, 5, 2)), dma((J, Q)), dma((J, Q)),
        ],
        compiler_params=pltpu.CompilerParams(
            collective_id=0, has_side_effects=True, vmem_limit_bytes=56 * 2**20
        ),
    )(sums, points, live_count, constants[0], linear(first_vectors), linear(second_vectors))
    return out.reshape(PAIRS, 1, B * B)


def solution(mesh):
    return jax.shard_map(
        body,
        mesh=mesh,
        in_specs=(
            P("row", "ba", None),
            P("row", None, "ba", None),
            P(),
            P("row"),
            P("row", None),
            P(),
            P("row", None),
            P("row", None, None),
            P("row", None, None),
        ),
        out_specs=P("row", "ba", None),
        check_vma=False,
    )
```

time: 361 us -> 108 us (0.30)
  blocking collectives: 171 us -> 0 us
  Pallas kernels: 0 us -> 99.2 us
  waiting for transfers between devices: 64.1 us -> 0 us
  matrix products: 46.2 us -> 0 us
  local copies, waits for them, and re-layouts: 47.9 us -> 3.06 us
  between operations: 15.1 us -> 1.33 us
  other arithmetic: 12.9 us -> 3.6 us
    psum x1 -> x0, blocking collectives: 128 us -> none  [broadcast(): return lax.psum(jnp.where(mine, shard, jnp.zeros_like(shard)), axis)]
    pallas_call x0 -> x1, Pallas kernels: none -> 99.2 us  [body(): pl.pallas_call(kernel, out_shape=jax.ShapeDtypeStruct((PAIRS, TILES, LANE...]
    unnamed x3 -> x0, waiting for transfers between devices: 49.3 us -> none
    dot_general x4 -> x0, matrix products: 46.2 us -> none  [the longest x1 26.1 us: body(): jnp.einsum('kuir,nirx->knux', rotation, shard_block, precision=HIGHEST)]
    all_gather x1 -> x0, blocking collectives: 43 us -> none  [body(): shard_geometry = lax.all_gather(geometry, 'row', axis=2, tiled=True)]
    slice x4 -> x0, local copies, waits for them, and re-layouts: 21.6 us -> none  [the longest x2 20.2 us: complex_block(): imag_part = vectors[:, 1].reshape(pair_count, branches, branches)]
    another operation x7 -> x0, local copies, waits for them, and re-layouts: 17 us -> none  [the longest x3 8.34 us: complex_block(): upper_row = jnp.stack([real_part, -imag_part], axis=1)]
    all_gather x1 -> x0, waiting for transfers between devices: 14.8 us -> none  [body(): shard_block = lax.all_gather(contracted, 'row', axis=2, tiled=True)]
  transfers between devices with their start and end apart: 2 -> 0, of which waited for: 2 -> 0; matrix products, arithmetic and copies ran while one was open for 14% -> 0% of each run, Pallas kernels for 0% -> 0%
where the time goes in v1:
time: 108 us; the launch traced here: 107 us
  Pallas kernels  99.2 us (92%)
  other arithmetic  3.6 us (3%)
  local copies, waits for them, and re-layouts  3.06 us (3%)
  between operations  1.33 us (1%)
    pallas_call x1, Pallas kernels, body(): pl.pallas_call(kernel, out_shape=jax.ShapeDtypeStruct((PAIRS, TILES, LANE...  99.2 us
    unnamed x2, local copies, waits for them, and re-layouts  2.45 us

profile of v1, /device:TPU:1, one launch (start us, length us, event | category | flops | bytes accessed | tf_op | source)
XLA Modules:
  0.0 107.2 jit_solution(15420177621220381905)
XLA Ops:
  1.3 1.4 %bitcast_subtract_fusion = (s32[3]{0:T(128)S(1)}, s32[]{:T(128)}) fusion(s32[1,6]{1,0:T(1,128)} %param.13, s32[3]{0:T(128)} %param.14), kind=kLoop, calls=%fused_computation.7 | loop fusion | flops 8 | bytes 52 | tf_op jit(solution)/shard_map/sub | solution.py:347
  2.8 0.7 add_convert_fusion
  3.5 0.7 convert_element_type.13
  4.2 0.1 copy.21
  4.2 0.1 broadcast_select_fusion
  4.3 0.6 pad.4.points_ref
  4.9 0.7 pad_maximum_fusion.sum_ref
  5.6 99.2 %shard_map.91 = f32[8,288,128]{2,1,0:T(8,128)} custom-call(f32[16,128]{1,0:T(8,128)} %pad_maximum_fusion.sum_ref, f32[16,128]{1,0:T(8,128)} %pad.4.points_ref, s32[1]{0:T(128)S(6)} %copy.24.live_ref, f32[48,36864]{1,0:T(8,128)} %bitcast.28, f32[8,576,128]{2,1,0:T(8,128)} %bitcast.30, f32[8,576,128]{2,1,0:T(8,128)} %bitcast.31), custom_call_target="tpu_custom_call" | custom-call | tf_op jit(solution)/shard_map/pallas_call | solution.py:358
  104.9 2.4 %copy.25 = f32[8,1,36864]{2,1,0:T(1,128)} copy(f32[8,1,36864]{2,1,0:T(1,128)} %bitcast.29) | data formatting | bytes 2359296
  (6 shorter events, 0.0 us)

commit v2 on v1

v2 whole, which is shorter than its diff:
```python
import functools
import math

import jax
import jax.numpy as jnp
from jax import lax
from jax.experimental import pallas as pl
from jax.experimental.pallas import tpu as pltpu
from jax.sharding import PartitionSpec as P

B = 192
G = 32
Z, X = 8, 4
Q = 2 * X
R = Z * Q
LANES = 128
TILES = B * B // LANES
SHARE = TILES // Q
J = 3
TT = SHARE // J
BLK = 2 * TT
HALF = Q // 2
PAIRS = 8
KO = 2 * PAIRS
MESH = pl.DeviceIdType.MESH
F32 = jnp.float32
BF16 = jnp.bfloat16


def split(value):
    high = value.astype(BF16)
    return high, (value - high.astype(F32)).astype(BF16)


def dot(a, b):
    return lax.dot_general(a, b, (((1,), (0,)), ((), ())), preferred_element_type=F32)


def dot3(ah, al, bh, bl):
    return dot(ah, bh) + dot(al, bh) + dot(ah, bl)


def kernel(
    modes_ref, owner_ref, live_ref, triplets_ref, center_ref, points_ref,
    const_ref, first_ref, second_ref, out_ref,
    modes_v, owner_s, live_s, triplets_s, center_s, points_v,
    const_v, first_v, second_v, tile, got1, got2, rot, lhs, term, part1, part2, final,
    gathered, phase_out, phase_in, square, first_t, second_m,
    small_sem, const_sem, second_sem, first_sem,
    s1, r1, s2, r2, sy1, ry1, sy2, ry2, sc, rc, sz, rz, sp, rp,
):
    row = lax.axis_index("row")
    y = lax.axis_index("ba")
    z = row // Q
    q = row % Q
    x = q // 2
    core = q % 2
    ya = y + 1 - 2 * (y % 2)
    yb = 3 - y
    y2 = (y + 2) % 4

    def qpeer(i):
        return ((x + i // 2) % X) * 2 + (core + i % 2) % 2

    def zpeer(i):
        return (z + i) % Z

    barrier = pltpu.get_barrier_semaphore()
    for i in range(1, Z):
        pl.semaphore_signal(barrier, inc=1, device_id=(zpeer(i) * Q + q, y), device_id_type=MESH)
    for i in range(1, Q):
        pl.semaphore_signal(barrier, inc=1, device_id=(z * Q + qpeer(i), y), device_id_type=MESH)
    for other in (ya, yb):
        pl.semaphore_signal(barrier, inc=1, device_id=(row, other), device_id_type=MESH)

    def local(src, dst, sem):
        copy = pltpu.make_async_copy(src, dst, sem)
        copy.start()
        return copy

    small = [
        local(src, dst, small_sem.at[n])
        for n, (src, dst) in enumerate((
            (modes_ref, modes_v), (owner_ref, owner_s), (live_ref, live_s),
            (triplets_ref, triplets_s), (center_ref, center_s), (points_ref, points_v),
        ))
    ]
    first_copies = [
        local(
            first_ref.at[:, p, pl.ds(j * BLK, BLK), :],
            first_v.at[j, :, pl.ds(p * BLK, BLK), :],
            first_sem.at[j, p],
        )
        for j in range(J) for p in range(Q)
    ]
    second_copy = local(second_ref, second_v, second_sem)
    const_copies = {
        (j, p): local(
            const_ref.at[:, pl.ds((p * SHARE + j * TT) * LANES, TT * LANES)],
            const_v.at[j, p],
            const_sem.at[j, p],
        )
        for j in range(J) for p in range(Q)
    }

    tile[...] = jnp.zeros_like(tile)
    for copy in small:
        copy.wait()
    mine = jnp.where(owner_s[0] == row, 1.0, 0.0)
    for n in range(4):
        for s in range(2):
            tile[2 * n + s : 2 * n + s + 1, 0:48] = modes_v[s, n : n + 1, :] * mine
    tile[0:8] = tile[0:8] + pltpu.roll(tile[0:8], 48, 1)
    second_cell = [triplets_s[0, 3 + axis] for axis in range(3)]
    numbers = [triplets_s[0, axis] - second_cell[axis] for axis in range(3)]
    shift = sum(second_cell[axis] * center_s[axis] for axis in range(3)) % G
    lane8 = lax.broadcasted_iota(jnp.int32, (8, LANES), 1)
    line8 = lax.broadcasted_iota(jnp.int32, (8, LANES), 0)
    geometry = jnp.zeros((8, LANES), jnp.int32)
    for n, number in enumerate(numbers + [shift]):
        geometry = jnp.where(line8 == n, number, geometry)
    tile[8:16] = jnp.where(lane8 % R == row, geometry.astype(F32), 0.0)
    tile[16:19, 0:PAIRS] = points_v[...].astype(F32)
    points = tile[16:24]
    low_group = jnp.where(lane8 < 4, points, 0.0)
    high_group = points - low_group
    tile[16:24] = (
        low_group + pltpu.roll(low_group, 4, 1) + pltpu.roll(high_group, 4, 1) + pltpu.roll(high_group, 8, 1)
    )
    pl.semaphore_wait(barrier, Z - 1 + Q - 1 + 2)

    def remote(src, dst, send, recv, device):
        return pltpu.make_async_remote_copy(
            src_ref=src, dst_ref=dst, send_sem=send, recv_sem=recv,
            device_id=device, device_id_type=MESH,
        )

    copies1 = []
    for i in range(1, Z):
        copy = remote(tile.at[0:16], got1.at[i], s1.at[i], r1.at[i], (zpeer(i) * Q + q, y))
        copy.start()
        copies1.append(copy)

    def paired(ref, k, start, stride):
        tiles = [ref[k, pl.ds(start + stride // 3 * i, B // 2, stride=stride), :] for i in range(3)]
        return both_parities(tiles)

    def both_parities(tiles):
        even = jnp.concatenate(tiles[0:2], axis=1)
        odd = pltpu.roll(jnp.concatenate(tiles[1:3], axis=1), 192, 1)
        return even, odd

    def prepare_second(k, carry):
        for o in range(2):
            even, odd = paired(second_v, k, o, 6)
            for i in range(2):
                lanes = slice(i * LANES, (i + 1) * LANES)
                square[i, pl.ds(0, B // 2, stride=2), :] = even[:, lanes]
                square[i, pl.ds(1, B // 2, stride=2), :] = odd[:, lanes]
            high, low = split(jnp.concatenate([square[0, 0:B, :], square[1, 0:B, :]], axis=1))
            zero = jnp.zeros((256 - B, 256), BF16)
            second_m[k, o, 0] = jnp.concatenate([high, zero], axis=0)
            second_m[k, o, 1] = jnp.concatenate([low, zero], axis=0)
        return carry

    def prepare_first(k, carry):
        for o in range(2):
            lines = []
            for j in range(J):
                lines += both_parities(
                    [first_v[j, k, pl.ds(2 * i + o, B // 2 // J, stride=6), :] for i in range(3)]
                )
            zero = jnp.zeros((256 - B, 256), F32)
            turned = jnp.transpose(jnp.concatenate(lines + [zero], axis=0))
            for i in range(2):
                lanes = slice(i * LANES, (i + 1) * LANES)
                square[i] = turned[:, lanes]
                for parity in range(2):
                    high, low = split(square[i, pl.ds(parity, B // 2, stride=2), :])
                    rows = slice(parity * (B // 2), (parity + 1) * (B // 2))
                    first_t[k, o, 0, rows, lanes] = high
                    first_t[k, o, 1, rows, lanes] = low
        return carry

    for copy in first_copies:
        copy.wait()
    lax.fori_loop(0, PAIRS, prepare_first, 0)
    for copy in copies1:
        copy.wait_recv()
    total = tile[0:16]
    for i in range(1, Z):
        total = total + got1[i]
    got2[q, 0:16] = total
    got2[q, 16:24] = tile[16:24]
    copies2 = []
    for i in range(1, Q):
        copy = remote(got2.at[q], got2.at[q], s2.at[i], r2.at[i], (z * Q + qpeer(i), y))
        copy.start()
        copies2.append(copy)
    second_copy.wait()
    lax.fori_loop(0, PAIRS, prepare_second, 0)

    for copy in copies2:
        copy.wait_recv()
    total = got2[0, 0:16]
    points = got2[0, 16:24]
    for i in range(1, Q):
        total = total + got2[i, 0:16]
        points = points + pltpu.roll(got2[i, 16:24], KO * i, 1)
    points = jnp.where(line8 == 3, -1.0, points)
    turns = lax.dot_general(
        points, total[8:16], (((0,), (0,)), ((), ())), preferred_element_type=F32
    )
    lane = lax.broadcasted_iota(jnp.int32, (Q * KO, LANES), 1)
    line = lax.broadcasted_iota(jnp.int32, (Q * KO, LANES), 0)
    turns = turns + jnp.where(lane >= R, 8.0, 0.0) - jnp.where(line % 8 >= 4, 8.0, 0.0)
    turns = turns - G * jnp.floor(turns * (1.0 / G))
    high, low = split(jnp.cos(turns * (2.0 * math.pi / G)))
    rot[:, 0:128] = high
    rot[:, 128:256] = low
    eigen = total[0:8] * jnp.where(live_s[0] > 0, 1.0, 0.0)
    high, low = split(eigen)
    lhs[...] = jnp.concatenate(
        [high.astype(F32), jnp.where(lane8 < 48, low.astype(F32), 0.0)], axis=0
    ).astype(BF16)

    def contract(j):
        def step(p, carry):
            pltpu.make_async_copy(const_ref.at[:, pl.ds(0, TT * LANES)], const_v.at[j, p], const_sem.at[j, p]).wait()
            high, low = split(const_v[j, p])
            both = dot(lhs[:, 0:96], jnp.concatenate([high, low], axis=0))
            both = both[0:8] + both[8:16]
            for t in range(TT):
                term[j, p, pl.ds(t, 8, stride=TT), :] = both[:, t * LANES : (t + 1) * LANES]
            return carry

        lax.fori_loop(0, Q, step, 0)

    waits = []

    def go(copy):
        copy.start()
        waits.append(copy)
        return copy

    def band(j, h, n):
        return term.at[j, pl.ds(HALF * h, HALF), pl.ds(pl.multiple_of(n * BLK, 8), BLK), :]

    y1, yy2, c2a, ring, p2a = {}, {}, {}, {}, {}

    def y1_start(j):
        for h, other in enumerate((ya, yb)):
            for slot, n in enumerate((other, y2)):
                y1[j, h, slot] = go(remote(
                    band(j, h, n), part1.at[j, h, slot], sy1.at[j, h, slot], ry1.at[j, h, slot], (row, other)
                ))

    def y2_start(j):
        for h, other in enumerate((yb, ya)):
            y1[j, h, 1].wait_recv()
            mine = band(j, h, other)
            mine[...] = mine[...] + part1[j, h, 1]
            yy2[j, h] = go(remote(mine, part2.at[j, h], sy2.at[j, h], ry2.at[j, h], (row, other)))

    def slot_rows(r, count=1):
        return pl.ds(pl.multiple_of(r * BLK, 8), count * BLK)

    def c2a_start(j):
        for h in range(2):
            y1[j, h, 0].wait_recv()
            yy2[j, h].wait_recv()
            final[j, HALF * h : HALF * (h + 1)] = band(j, h, y)[...] + part1[j, h, 0] + part2[j, h]
        gathered[j, slot_rows(row), :] = final[j, q]
        for i in range(1, Q):
            c2a[j, i] = go(remote(
                final.at[j, qpeer(i)], gathered.at[j, slot_rows(row), :], sc.at[j, i], rc.at[j, i],
                (z * Q + qpeer(i), y),
            ))

    def ring_start(j, i):
        for h in range(2):
            if i == 1 and h == 0:
                for n in range(1, Q):
                    c2a[j, n].wait_recv()
            elif i > 1:
                for side in range(2):
                    ring[j, i - 1, side, h].wait_recv()
            for side, sign in enumerate((1, -1)):
                if i == 4 and side != h:
                    continue
                base = ((z + Z - sign * (i - 1)) % Z) * Q + HALF * h
                block = gathered.at[j, slot_rows(base, HALF), :]
                ring[j, i, side, h] = go(remote(
                    block, block, sz.at[j, i, side, h], rz.at[j, i, side, h],
                    (((z + Z + sign) % Z) * Q + q, y),
                ))

    def phase(j):
        for side in range(2):
            ring[j, 4, side, side].wait_recv()

        def step(u, carry):
            cols = []
            for v in range(2):
                t = 2 * u + v
                cols.append(jnp.concatenate(
                    [gathered[j, pl.ds(s * TT + t, R, stride=BLK), :] for s in range(2)], axis=0
                ))
            high, low = split(jnp.concatenate(cols, axis=1))
            value = dot(rot[...], jnp.concatenate([high, high], axis=0)) + dot(rot[:, 0:128], low)
            for v in range(2):
                for d in range(2 * Q):
                    phase_out[j, d % 2, d // 2, pl.ds(pl.multiple_of((2 * u + v) * 8, 8), 8), :] = value[
                        d * 8 : (d + 1) * 8, v * LANES : (v + 1) * LANES
                    ]
            return carry

        lax.fori_loop(0, TT // 2, step, 0)
        rows = pl.ds(pl.multiple_of(q * TT * 8, 8), TT * 8)
        for g in range(2):
            for i in range(1, Q):
                p2a[j, g, i] = go(remote(
                    phase_out.at[j, g, qpeer(i)], phase_in.at[j, g, rows, :], sp.at[j, g, i], rp.at[j, g, i],
                    (z * Q + qpeer(i), y),
                ))
            phase_in[j, g, rows, :] = phase_out[j, g, q]

    contract(0)
    y1_start(0)
    contract(1)
    y1_start(1)
    y2_start(0)
    contract(2)
    y1_start(2)
    y2_start(1)
    c2a_start(0)
    y2_start(2)
    ring_start(0, 1)
    c2a_start(1)
    ring_start(0, 2)
    c2a_start(2)
    ring_start(0, 3)
    ring_start(1, 1)
    ring_start(0, 4)
    ring_start(1, 2)
    phase(0)
    ring_start(1, 3)
    ring_start(2, 1)
    ring_start(1, 4)
    ring_start(2, 2)
    phase(1)
    ring_start(2, 3)
    ring_start(2, 4)
    phase(2)

    def finish(k, carry):
        g = k // 4
        planes = []
        for o in range(2):
            lines = []
            for j in range(J):
                lines += both_parities([
                    phase_in[j, g, pl.ds(8 * i + 4 * o + k % 4, B // 2 // J, stride=24), :]
                    for i in range(3)
                ])
            planes.append(split(jnp.concatenate(lines, axis=0)))
        (prh, prl), (pih, pil) = planes
        wr = (second_m[k, 0, 0], second_m[k, 0, 1])
        wi = (second_m[k, 1, 0], second_m[k, 1, 1])
        real = dot3(prh, prl, *wr) - dot3(pih, pil, *wi)
        imag = dot3(prh, prl, *wi) + dot3(pih, pil, *wr)
        zero = jnp.zeros((256 - B, 256), F32)
        tr = split(jnp.concatenate([real, zero], axis=0))
        ti = split(jnp.concatenate([imag, zero], axis=0))
        vr = (first_t[k, 0, 0], first_t[k, 0, 1])
        vi = (first_t[k, 1, 0], first_t[k, 1, 1])
        real = dot3(*vr, *tr) - dot3(*vi, *ti)
        imag = dot3(*vr, *ti) + dot3(*vi, *tr)
        value = (real * real + imag * imag) * (1.0 / R)
        even = value[0 : B // 2]
        odd = pltpu.roll(value[B // 2 : B], 64, 1)
        lane = lax.broadcasted_iota(jnp.int32, (B // 2, LANES), 1)
        out_ref[k, pl.ds(0, B // 2, stride=3), :] = even[:, 0:LANES]
        out_ref[k, pl.ds(1, B // 2, stride=3), :] = jnp.where(
            lane < 64, even[:, LANES:], odd[:, 0:LANES]
        )
        out_ref[k, pl.ds(2, B // 2, stride=3), :] = odd[:, LANES:]
        return carry

    for g in range(2):
        for j in range(J):
            for i in range(1, Q):
                p2a[j, g, i].wait_recv()
        lax.fori_loop(4 * g, 4 * g + 4, finish, 0)
    for copy in copies1 + copies2 + waits:
        copy.wait_send()


def linear(vectors):
    tiles = vectors.reshape(PAIRS, 2, TILES, LANES)
    return tiles.transpose(0, 2, 1, 3).reshape(PAIRS, 2 * TILES, LANES)


def body(
    constants,
    current_modes,
    owner_id,
    live_count,
    triplets,
    center_point,
    pair_points,
    first_vectors,
    second_vectors,
):
    anywhere = pl.BlockSpec(memory_space=pltpu.HBM)
    dma = pltpu.SemaphoreType.DMA
    out = pl.pallas_call(
        kernel,
        out_shape=jax.ShapeDtypeStruct((PAIRS, TILES, LANES), F32),
        in_specs=[anywhere] * 9,
        out_specs=pl.BlockSpec(memory_space=pltpu.VMEM),
        scratch_shapes=[
            pltpu.VMEM((2, 4, 48), F32),
            pltpu.SMEM((1,), jnp.int32),
            pltpu.SMEM((1,), jnp.int32),
            pltpu.SMEM((1, 6), jnp.int32),
            pltpu.SMEM((3,), jnp.int32),
            pltpu.VMEM((3, PAIRS), jnp.int32),
            pltpu.VMEM((J, Q, 48, TT * LANES), F32),
            pltpu.VMEM((J, PAIRS, Q * BLK, LANES), F32),
            pltpu.VMEM((PAIRS, 2 * TILES, LANES), F32),
            pltpu.VMEM((24, LANES), F32),
            pltpu.VMEM((Z, 16, LANES), F32),
            pltpu.VMEM((Q, 24, LANES), F32),
            pltpu.VMEM((Q * KO, 256), BF16),
            pltpu.VMEM((16, LANES), BF16),
            pltpu.VMEM((J, Q, 4 * BLK, LANES), F32),
            pltpu.VMEM((J, 2, 2, HALF, BLK, LANES), F32),
            pltpu.VMEM((J, 2, HALF, BLK, LANES), F32),
            pltpu.VMEM((J, Q, BLK, LANES), F32),
            pltpu.VMEM((J, R * BLK, LANES), F32),
            pltpu.VMEM((J, 2, Q, TT * 8, LANES), F32),
            pltpu.VMEM((J, 2, Q * TT * 8, LANES), F32),
            pltpu.VMEM((2, 256, LANES), F32),
            pltpu.VMEM((PAIRS, 2, 2, B, 256), BF16),
            pltpu.VMEM((PAIRS, 2, 2, 256, 256), BF16),
            dma((6,)), dma((J, Q)), dma, dma((J, Q)),
            dma((Z,)), dma((Z,)), dma((Q,)), dma((Q,)),
            dma((J, 2, 2)), dma((J, 2, 2)), dma((J, 2)), dma((J, 2)),
            dma((J, Q)), dma((J, Q)), dma((J, 5, 2, 2)), dma((J, 5, 2, 2)),
            dma((J, 2, Q)), dma((J, 2, Q)),
        ],
        compiler_params=pltpu.CompilerParams(
            collective_id=0, has_side_effects=True, vmem_limit_bytes=60 * 2**20
        ),
    )(
        current_modes[0].transpose(0, 2, 1), owner_id, live_count, triplets, center_point, pair_points.T,
        constants[0], linear(first_vectors).reshape(PAIRS, Q, 2 * SHARE, LANES), linear(second_vectors),
    )
    return out.reshape(PAIRS, 1, B * B)


def solution(mesh):
    return jax.shard_map(
        body,
        mesh=mesh,
        in_specs=(
            P("row", "ba", None),
            P("row", None, "ba", None),
            P(),
            P("row"),
            P("row", None),
            P(),
            P("row", None),
            P("row", None, None),
            P("row", None, None),
        ),
        out_specs=P("row", "ba", None),
        check_vma=False,
    )
```

time: 108 us -> 93.4 us (0.86)
  Pallas kernels: 99.2 us -> 89.7 us
  other arithmetic: 3.6 us -> 0 us
    pallas_call x1, Pallas kernels: 99.2 us -> 89.7 us  [body(): pl.pallas_call(kernel, out_shape=jax.ShapeDtypeStruct((PAIRS, TILES, LANE...]
    sub x1 -> x0, other arithmetic: 1.44 us -> none  [body(): offsets = triplets[0, 0:3] - second_cell]
    convert_element_type x2 -> x0, other arithmetic: 1.41 us -> none  [the longest x1 0.72 us: body(): jnp.concatenate([offsets, shift[None], jnp.zeros((4,), jnp.int32)])]
    unnamed x2 -> x1, local copies, waits for them, and re-layouts: 2.45 us -> 2.37 us
where the time goes in v2:
time: 93.4 us; the launch traced here: 93.3 us
  Pallas kernels  89.7 us (96%)
  local copies, waits for them, and re-layouts  2.37 us (3%)
  between operations  1.3 us (1%)
    pallas_call x1, Pallas kernels, body(): pl.pallas_call(kernel, out_shape=jax.ShapeDtypeStruct((PAIRS, TILES, LANE...  89.7 us
    unnamed x1, local copies, waits for them, and re-layouts  2.37 us

profile of v2, /device:TPU:1, one launch (start us, length us, event | category | flops | bytes accessed | tf_op | source)
XLA Modules:
  0.0 93.3 jit_solution(8453995637342436204)
XLA Ops:
  1.3 89.7 %shard_map.91 = f32[8,288,128]{2,1,0:T(8,128)} custom-call(f32[2,4,48]{2,1,0:T(4,128)} %bitcast.20, s32[1]{0:T(128)S(6)} %copy.14.owner_ref, s32[1]{0:T(128)S(6)} %copy.15.live_ref, s32[1,6]{1,0:T(1,128)} %triplets_ref.1, s32[3]{0:T(128)} %center_ref.1, s32[3,8]{1,0:T(4,128)} %bitcast.21, f32[48,36864]{1,0:T(8,128)} %bitcast.16, f32[8,8,72,128]{3,2,1,0:T(8,128)} %bitcast.18, ...), custom_call_target="tpu_custom_call" | custom-call | tf_op jit(solution)/shard_map/pallas_call | solution.py:417
  91.0 2.4 %copy.16 = f32[8,1,36864]{2,1,0:T(1,128)} copy(f32[8,1,36864]{2,1,0:T(1,128)} %bitcast.17) | data formatting | bytes 2359296

commit v3 on v2

v3 whole, which is shorter than its diff:
```python
import functools
import math

import jax
import jax.numpy as jnp
from jax import lax
from jax.experimental import pallas as pl
from jax.experimental.pallas import tpu as pltpu
from jax.sharding import PartitionSpec as P

B = 192
G = 32
Z, X = 8, 4
Q = 2 * X
R = Z * Q
LANES = 128
TILES = B * B // LANES
SHARE = TILES // Q
PIECES = (8, 8, 8, 12)
J = len(PIECES)
ORDER = (
    "C0", "Y0", "C1", "Y1", "C2", "Y2", "A0", "A1", "a0", "C3", "Y3", "A2",
    "11", "12", "21", "b0", "A3", "22", "31", "13", "P0", "41", "32", "23",
    "P1", "42", "33", "P2", "43", "P3",
)
STARTS = tuple(sum(PIECES[:j]) for j in range(J))
HALF = Q // 2
FAST = 1
PAIRS = 8
KO = 2 * PAIRS
MESH = pl.DeviceIdType.MESH
F32 = jnp.float32
BF16 = jnp.bfloat16


def split(value):
    high = value.astype(BF16)
    return high, (value - high.astype(F32)).astype(BF16)


def dot(a, b):
    return lax.dot_general(a, b, (((1,), (0,)), ((), ())), preferred_element_type=F32)


def dot3(ah, al, bh, bl):
    return dot(ah, bh) + dot(al, bh) + dot(ah, bl)


def kernel(
    modes_ref, owner_ref, live_ref, triplets_ref, center_ref, points_ref,
    const_ref, first_ref, second_ref, out_ref,
    modes_v, owner_s, live_s, triplets_s, center_s, points_v,
    const_v, first_v, second_v, tile, got1, got2, rot, lhs, term, part, final,
    gathered, phase_out, phase_in, square, first_t, second_m, out_v,
    out_sem, small_sem, const_sem, second_sem, first_sem,
    s1, r1, s2, r2, sy, ry, sc, rc, sz, rz, sp, rp,
):
    row = lax.axis_index("row")
    y = lax.axis_index("ba")
    z = row // Q
    q = row % Q
    x = q // 2
    core = q % 2

    def qpeer(i):
        return ((x + i // 2) % X) * 2 + (core + i % 2) % 2

    def zpeer(i):
        return (z + i) % Z

    barrier = pltpu.get_barrier_semaphore()
    for i in range(1, Z):
        pl.semaphore_signal(barrier, inc=1, device_id=(zpeer(i) * Q + q, y), device_id_type=MESH)
    for i in range(1, Q):
        pl.semaphore_signal(barrier, inc=1, device_id=(z * Q + qpeer(i), y), device_id_type=MESH)
    for i in range(1, 4):
        pl.semaphore_signal(barrier, inc=1, device_id=(row, (y + i) % 4), device_id_type=MESH)

    def local(src, dst, sem):
        copy = pltpu.make_async_copy(src, dst, sem)
        copy.start()
        return copy

    small = [
        local(src, dst, small_sem.at[n])
        for n, (src, dst) in enumerate((
            (modes_ref, modes_v), (owner_ref, owner_s), (live_ref, live_s),
            (triplets_ref, triplets_s), (center_ref, center_s), (points_ref, points_v),
        ))
    ]
    const_copies = {
        (j, p): local(
            const_ref.at[:, pl.ds((p * SHARE + STARTS[j]) * LANES, PIECES[j] * LANES)],
            const_v.at[p, :, pl.ds(STARTS[j] * LANES, PIECES[j] * LANES)],
            const_sem.at[j, p],
        )
        for j in range(J) for p in range(Q)
    }
    first_copy = local(first_ref, first_v, first_sem)
    second_copy = local(second_ref, second_v, second_sem)

    tile[...] = jnp.zeros_like(tile)
    for copy in small:
        copy.wait()
    mine = jnp.where(owner_s[0] == row, 1.0, 0.0)
    for n in range(4):
        for s in range(2):
            tile[2 * n + s : 2 * n + s + 1, 0:48] = modes_v[s, n : n + 1, :] * mine
    tile[0:8] = tile[0:8] + pltpu.roll(tile[0:8], 48, 1)
    second_cell = [triplets_s[0, 3 + axis] for axis in range(3)]
    numbers = [triplets_s[0, axis] - second_cell[axis] for axis in range(3)]
    shift = sum(second_cell[axis] * center_s[axis] for axis in range(3)) % G
    lane8 = lax.broadcasted_iota(jnp.int32, (8, LANES), 1)
    line8 = lax.broadcasted_iota(jnp.int32, (8, LANES), 0)
    geometry = jnp.zeros((8, LANES), jnp.int32)
    for n, number in enumerate(numbers + [shift]):
        geometry = jnp.where(line8 == n, number, geometry)
    tile[8:16] = jnp.where(lane8 % R == row, geometry.astype(F32), 0.0)
    tile[16:19, 0:PAIRS] = points_v[...].astype(F32)
    points = tile[16:24]
    low_group = jnp.where(lane8 < 4, points, 0.0)
    high_group = points - low_group
    tile[16:24] = (
        low_group + pltpu.roll(low_group, 4, 1) + pltpu.roll(high_group, 4, 1) + pltpu.roll(high_group, 8, 1)
    )
    pl.semaphore_wait(barrier, Z - 1 + Q - 1 + 3)

    def remote(src, dst, send, recv, device):
        return pltpu.make_async_remote_copy(
            src_ref=src, dst_ref=dst, send_sem=send, recv_sem=recv,
            device_id=device, device_id_type=MESH,
        )

    copies1 = []
    for i in range(1, Z):
        copy = remote(tile.at[0:16], got1.at[i], s1.at[i], r1.at[i], (zpeer(i) * Q + q, y))
        copy.start()
        copies1.append(copy)

    def paired(ref, k, start, stride):
        tiles = [ref[k, pl.ds(start + stride // 3 * i, B // 2, stride=stride), :] for i in range(3)]
        return both_parities(tiles)

    def both_parities(tiles):
        even = jnp.concatenate(tiles[0:2], axis=1)
        odd = pltpu.roll(jnp.concatenate(tiles[1:3], axis=1), 192, 1)
        return even, odd

    def prepare_second(k, carry):
        for o in range(2):
            even, odd = paired(second_v, k, o, 6)
            for i in range(2):
                lanes = slice(i * LANES, (i + 1) * LANES)
                square[i, pl.ds(0, B // 2, stride=2), :] = even[:, lanes]
                square[i, pl.ds(1, B // 2, stride=2), :] = odd[:, lanes]
            high, low = split(jnp.concatenate([square[0, 0:B, :], square[1, 0:B, :]], axis=1))
            zero = jnp.zeros((256 - B, 256), BF16)
            second_m[k, o, 0] = jnp.concatenate([high, zero], axis=0)
            second_m[k, o, 1] = jnp.concatenate([low, zero], axis=0)
        return carry

    def prepare_first(k, carry):
        for o in range(2):
            even, odd = paired(first_v, k, o, 6)
            zero = jnp.zeros((256 - B, 256), F32)
            turned = jnp.transpose(jnp.concatenate([even, odd, zero], axis=0))
            for i in range(2):
                lanes = slice(i * LANES, (i + 1) * LANES)
                square[i] = turned[:, lanes]
                for parity in range(2):
                    high, low = split(square[i, pl.ds(parity, B // 2, stride=2), :])
                    rows = slice(parity * (B // 2), (parity + 1) * (B // 2))
                    first_t[k, o, 0, rows, lanes] = high
                    first_t[k, o, 1, rows, lanes] = low
        return carry

    for copy in copies1:
        copy.wait_recv()
    total = tile[0:16]
    for i in range(1, Z):
        total = total + got1[i]
    got2[q, 0:16] = total
    got2[q, 16:24] = tile[16:24]
    copies2 = []
    for i in range(1, Q):
        copy = remote(got2.at[q], got2.at[q], s2.at[i], r2.at[i], (z * Q + qpeer(i), y))
        copy.start()
        copies2.append(copy)

    for copy in copies2:
        copy.wait_recv()
    total = got2[0, 0:16]
    points = got2[0, 16:24]
    for i in range(1, Q):
        total = total + got2[i, 0:16]
        points = points + pltpu.roll(got2[i, 16:24], KO * i, 1)
    eigen = total[0:8] * jnp.where(live_s[0] > 0, 1.0, 0.0)
    high, low = split(eigen)
    lhs[...] = jnp.concatenate(
        [high.astype(F32), jnp.where(lane8 < 48, low.astype(F32), 0.0)], axis=0
    ).astype(BF16)

    def rotation():
        turns = lax.dot_general(
            jnp.where(line8 == 3, -1.0, points), total[8:16], (((0,), (0,)), ((), ())),
            preferred_element_type=F32,
        )
        lane = lax.broadcasted_iota(jnp.int32, (Q * KO, LANES), 1)
        line = lax.broadcasted_iota(jnp.int32, (Q * KO, LANES), 0)
        turns = turns + jnp.where(lane >= R, 8.0, 0.0) - jnp.where(line % 8 >= 4, 8.0, 0.0)
        turns = turns - G * jnp.floor(turns * (1.0 / G))
        high, low = split(jnp.cos(turns * (2.0 * math.pi / G)))
        rot[:, 0:128] = high
        rot[:, 128:256] = low

    def contract(j):
        tiles = PIECES[j]
        lanes = slice(STARTS[j] * LANES, (STARTS[j] + tiles) * LANES)

        def step(p, carry):
            pltpu.make_async_copy(
                const_ref.at[:, pl.ds(0, tiles * LANES)], const_v.at[p, :, lanes], const_sem.at[j, p]
            ).wait()
            high, low = split(const_v[p, :, lanes])
            both = dot(lhs[:, 0:96], jnp.concatenate([high, low], axis=0))
            both = both[0:8] + both[8:16]
            for t in range(tiles):
                term[p, pl.ds(8 * STARTS[j] + t, 8, stride=tiles), :] = both[:, t * LANES : (t + 1) * LANES]
            return carry

        lax.fori_loop(0, Q, step, 0)

    waits = []

    def go(copy):
        copy.start()
        waits.append(copy)
        return copy

    def rows(j):
        return pl.ds(2 * STARTS[j], 2 * PIECES[j])

    def band(j, n):
        start = pl.multiple_of(8 * STARTS[j] + n * (2 * PIECES[j]), 8)
        return term.at[:, pl.ds(start, 2 * PIECES[j]), :]

    yx, c2a, ring, p2a = {}, {}, {}, {}

    def y_start(j):
        for i in range(1, 4):
            other = (y + i) % 4
            yx[j, i] = go(remote(
                band(j, other), part.at[i, :, rows(j), :], sy.at[j, i], ry.at[j, i], (row, other)
            ))

    def slot_rows(j, r, count=1):
        block = 2 * PIECES[j]
        return pl.ds(pl.multiple_of(R * 2 * STARTS[j] + r * block, 8), count * block)

    def c2a_start(j):
        for i in range(1, 4):
            yx[j, i].wait_recv()
        final[:, rows(j), :] = (
            band(j, y)[...] + part[1, :, rows(j), :] + part[2, :, rows(j), :] + part[3, :, rows(j), :]
        )
        for i in range(1, Q):
            c2a[j, i] = go(remote(
                final.at[qpeer(i), rows(j), :], gathered.at[slot_rows(j, row), :],
                sc.at[j, i], rc.at[j, i], (z * Q + qpeer(i), y),
            ))
        gathered[slot_rows(j, row), :] = final[q, rows(j), :]

    def ring_start(j, i):
        if i == 1:
            for n in range(1, Q):
                c2a[j, n].wait_recv()
        else:
            for side in range(2):
                ring[j, i - 1, side].wait_recv()
        for side, sign in enumerate((1, -1)):
            base = ((z + Z - sign * (i - 1)) % Z) * Q
            block = gathered.at[
                slot_rows(j, base, Q) if i < 4 else slot_rows(j, base + HALF * side, HALF), :
            ]
            ring[j, i, side] = go(remote(
                block, block, sz.at[j, i, side], rz.at[j, i, side], (((z + Z + sign) % Z) * Q + q, y)
            ))

    def ring_send(j, n, side, origin, hops, half=None):
        sign = 1 - 2 * side
        base = ((z + Z - sign * origin) % Z) * Q
        block = gathered.at[
            slot_rows(j, base, Q) if half is None else slot_rows(j, base + HALF * half, HALF), :
        ]
        ring[j, n, side] = go(remote(
            block, block, sz.at[j, n, side], rz.at[j, n, side], (((z + Z + sign * hops) % Z) * Q + q, y)
        ))

    def near_start(j):
        for n in range(1, Q):
            c2a[j, n].wait_recv()
        for hops in (2, 1):
            for side in range(2):
                ring_send(j, hops, side, 0, hops)

    def far_start(j):
        for side in range(2):
            ring[j, 2, side].wait_recv()
        for side in range(2):
            ring_send(j, 4, side, 2, 2, side)
        for side in range(2):
            ring_send(j, 3, side, 2, 1)

    def phase(j):
        tiles = PIECES[j]
        for n in (1, 3, 4) if j < FAST else (4,):
            for side in range(2):
                ring[j, n, side].wait_recv()

        def step(u, carry):
            cols = []
            for v in range(2):
                start = R * 2 * STARTS[j] + 2 * u + v
                cols.append(jnp.concatenate(
                    [gathered[pl.ds(start + s * tiles, R, stride=2 * tiles), :] for s in range(2)], axis=0
                ))
            high, low = split(jnp.concatenate(cols, axis=1))
            value = dot(rot[...], jnp.concatenate([high, high], axis=0)) + dot(rot[:, 0:128], low)
            for v in range(2):
                for d in range(2 * Q):
                    where = pl.ds(pl.multiple_of((STARTS[j] + 2 * u + v) * 8, 8), 8)
                    phase_out[d % 2, d // 2, where, :] = value[
                        d * 8 : (d + 1) * 8, v * LANES : (v + 1) * LANES
                    ]
            return carry

        lax.fori_loop(0, tiles // 2, step, 0)
        mine = pl.ds(STARTS[j] * 8, tiles * 8)
        there = pl.ds(pl.multiple_of((q * SHARE + STARTS[j]) * 8, 8), tiles * 8)
        for g in range(2) if j == J - 1 else (slice(None),):
            n = g if j == J - 1 else 0
            for i in range(1, Q):
                p2a[j, n, i] = go(remote(
                    phase_out.at[g, qpeer(i), mine, :], phase_in.at[g, there, :],
                    sp.at[j, n, i], rp.at[j, n, i], (z * Q + qpeer(i), y),
                ))
        for g in range(2):
            phase_in[g, there, :] = phase_out[g, q, mine, :]

    steps = {
        "C": contract, "Y": y_start, "A": c2a_start, "P": phase, "a": near_start, "b": far_start,
        **{str(i): functools.partial(ring_start, i=i) for i in range(1, 5)},
    }
    for name in ORDER:
        steps[name[0]](int(name[1]))
        if name in ("a0", "10"):
            rotation()
    first_copy.wait()
    lax.fori_loop(0, PAIRS, prepare_first, 0)
    second_copy.wait()
    lax.fori_loop(0, PAIRS, prepare_second, 0)
    late = 2 * (Q - 1)
    for copy in copies1 + copies2 + waits[:-late]:
        copy.wait_send()

    def finish(k, carry):
        g = k // 4
        planes = []
        for o in range(2):
            lines = both_parities(
                [phase_in[g, pl.ds(8 * i + 4 * o + k % 4, B // 2, stride=24), :] for i in range(3)]
            )
            planes.append(split(jnp.concatenate(lines, axis=0)))
        (prh, prl), (pih, pil) = planes
        wr = (second_m[k, 0, 0], second_m[k, 0, 1])
        wi = (second_m[k, 1, 0], second_m[k, 1, 1])
        real = dot3(prh, prl, *wr) - dot3(pih, pil, *wi)
        imag = dot3(prh, prl, *wi) + dot3(pih, pil, *wr)
        zero = jnp.zeros((256 - B, 256), F32)
        tr = split(jnp.concatenate([real, zero], axis=0))
        ti = split(jnp.concatenate([imag, zero], axis=0))
        vr = (first_t[k, 0, 0], first_t[k, 0, 1])
        vi = (first_t[k, 1, 0], first_t[k, 1, 1])
        real = dot3(*vr, *tr) - dot3(*vi, *ti)
        imag = dot3(*vr, *ti) + dot3(*vi, *tr)
        value = (real * real + imag * imag) * (1.0 / R)
        even = value[0 : B // 2]
        odd = pltpu.roll(value[B // 2 : B], 64, 1)
        lane = lax.broadcasted_iota(jnp.int32, (B // 2, LANES), 1)
        out_v[k, pl.ds(0, B // 2, stride=3), :] = even[:, 0:LANES]
        out_v[k, pl.ds(1, B // 2, stride=3), :] = jnp.where(
            lane < 64, even[:, LANES:], odd[:, 0:LANES]
        )
        out_v[k, pl.ds(2, B // 2, stride=3), :] = odd[:, LANES:]
        return carry

    outs = []
    for j in range(J - 1):
        for i in range(1, Q):
            p2a[j, 0, i].wait_recv()
    for g in range(2):
        for i in range(1, Q):
            p2a[J - 1, g, i].wait_recv()
        lax.fori_loop(4 * g, 4 * g + 4, finish, 0)
        outs.append(local(out_v.at[4 * g : 4 * g + 4], out_ref.at[4 * g : 4 * g + 4], out_sem.at[g]))
    for copy in waits[-late:]:
        copy.wait_send()
    for copy in outs:
        copy.wait()


def linear(vectors):
    tiles = vectors.reshape(PAIRS, 2, TILES, LANES)
    return tiles.transpose(0, 2, 1, 3).reshape(PAIRS, 2 * TILES, LANES)


def body(
    constants,
    current_modes,
    owner_id,
    live_count,
    triplets,
    center_point,
    pair_points,
    first_vectors,
    second_vectors,
):
    anywhere = pl.BlockSpec(memory_space=pltpu.HBM)
    dma = pltpu.SemaphoreType.DMA
    out = pl.pallas_call(
        kernel,
        out_shape=jax.ShapeDtypeStruct((PAIRS, TILES, LANES), F32),
        in_specs=[anywhere] * 9,
        out_specs=anywhere,
        scratch_shapes=[
            pltpu.VMEM((2, 4, 48), F32),
            pltpu.SMEM((1,), jnp.int32),
            pltpu.SMEM((1,), jnp.int32),
            pltpu.SMEM((1, 6), jnp.int32),
            pltpu.SMEM((3,), jnp.int32),
            pltpu.VMEM((3, PAIRS), jnp.int32),
            pltpu.VMEM((Q, 48, SHARE * LANES), F32),
            pltpu.VMEM((PAIRS, 2 * TILES, LANES), F32),
            pltpu.VMEM((PAIRS, 2 * TILES, LANES), F32),
            pltpu.VMEM((24, LANES), F32),
            pltpu.VMEM((Z, 16, LANES), F32),
            pltpu.VMEM((Q, 24, LANES), F32),
            pltpu.VMEM((Q * KO, 256), BF16),
            pltpu.VMEM((16, LANES), BF16),
            pltpu.VMEM((Q, 8 * SHARE, LANES), F32),
            pltpu.VMEM((4, Q, 2 * SHARE, LANES), F32),
            pltpu.VMEM((Q, 2 * SHARE, LANES), F32),
            pltpu.VMEM((R * 2 * SHARE, LANES), F32),
            pltpu.VMEM((2, Q, SHARE * 8, LANES), F32),
            pltpu.VMEM((2, Q * SHARE * 8, LANES), F32),
            pltpu.VMEM((2, 256, LANES), F32),
            pltpu.VMEM((PAIRS, 2, 2, B, 256), BF16),
            pltpu.VMEM((PAIRS, 2, 2, 256, 256), BF16),
            pltpu.VMEM((PAIRS, TILES, LANES), F32),
            dma((2,)), dma((6,)), dma((J, Q)), dma, dma,
            dma((Z,)), dma((Z,)), dma((Q,)), dma((Q,)),
            dma((J, 4)), dma((J, 4)),
            dma((J, Q)), dma((J, Q)), dma((J, 5, 2)), dma((J, 5, 2)),
            dma((J, 2, Q)), dma((J, 2, Q)),
        ],
        compiler_params=pltpu.CompilerParams(
            collective_id=0, has_side_effects=True, vmem_limit_bytes=60 * 2**20
        ),
    )(
        current_modes[0].transpose(0, 2, 1), owner_id, live_count, triplets, center_point, pair_points.T,
        constants[0], linear(first_vectors), linear(second_vectors),
    )
    return out.reshape(PAIRS, 1, B * B)


def solution(mesh):
    return jax.shard_map(
        body,
        mesh=mesh,
        in_specs=(
            P("row", "ba", None),
            P("row", None, "ba", None),
            P(),
            P("row"),
            P("row", None),
            P(),
            P("row", None),
            P("row", None, None),
            P("row", None, None),
        ),
        out_specs=P("row", "ba", None),
        check_vma=False,
    )
```

time: 93.4 us -> 88.3 us (0.945)
  Pallas kernels: 89.7 us -> 84.5 us
    pallas_call x1, Pallas kernels: 89.7 us -> 84.5 us  [body(): pl.pallas_call(kernel, out_shape=jax.ShapeDtypeStruct((PAIRS, TILES, LANE...]
where the time goes in v3:
time: 88.3 us; the launch traced here: 88.2 us
  Pallas kernels  84.5 us (96%)
  local copies, waits for them, and re-layouts  2.37 us (3%)
  between operations  1.3 us (1%)
    pallas_call x1, Pallas kernels, body(): pl.pallas_call(kernel, out_shape=jax.ShapeDtypeStruct((PAIRS, TILES, LANE...  84.5 us
    unnamed x1, local copies, waits for them, and re-layouts  2.37 us

profile of v3, /device:TPU:1, one launch (start us, length us, event | category | flops | bytes accessed | tf_op | source)
XLA Modules:
  0.0 88.2 jit_solution(16953438899205003373)
XLA Ops:
  1.3 84.5 %shard_map.91 = f32[8,288,128]{2,1,0:T(8,128)} custom-call(f32[2,4,48]{2,1,0:T(4,128)} %bitcast.20, s32[1]{0:T(128)S(6)} %copy.14.owner_ref, s32[1]{0:T(128)S(6)} %copy.15.live_ref, s32[1,6]{1,0:T(1,128)} %triplets_ref.1, s32[3]{0:T(128)} %center_ref.1, s32[3,8]{1,0:T(4,128)} %bitcast.21, f32[48,36864]{1,0:T(8,128)} %bitcast.16, f32[8,576,128]{2,1,0:T(8,128)} %bitcast.18, ...), custom_call_target="tpu_custom_call" | custom-call | tf_op jit(solution)/shard_map/pallas_call | solution.py:430
  85.8 2.4 %copy.16 = f32[8,1,36864]{2,1,0:T(1,128)} copy(f32[8,1,36864]{2,1,0:T(1,128)} %bitcast.17) | data formatting | bytes 2359296

commit v4 on v3

--- a/solution.py
+++ b/solution.py
@@ -28,6 +28,9 @@
 FAST = 1
 PAIRS = 8
 KO = 2 * PAIRS
+GROUPS = 4
+EACH = PAIRS // GROUPS
+SPAN = 2 * EACH
 MESH = pl.DeviceIdType.MESH
 F32 = jnp.float32
 BF16 = jnp.bfloat16
@@ -118,11 +121,13 @@
     tile[8:16] = jnp.where(lane8 % R == row, geometry.astype(F32), 0.0)
     tile[16:19, 0:PAIRS] = points_v[...].astype(F32)
     points = tile[16:24]
-    low_group = jnp.where(lane8 < 4, points, 0.0)
-    high_group = points - low_group
-    tile[16:24] = (
-        low_group + pltpu.roll(low_group, 4, 1) + pltpu.roll(high_group, 4, 1) + pltpu.roll(high_group, 8, 1)
-    )
+    spread = jnp.zeros((8, LANES), F32)
+    for g in range(GROUPS):
+        group = jnp.where(lane8 // EACH == g, points, 0.0)
+        for o in range(2):
+            by = g * EACH + o * EACH
+            spread = spread + (pltpu.roll(group, by, 1) if by else group)
+    tile[16:24] = spread
     pl.semaphore_wait(barrier, Z - 1 + Q - 1 + 3)
 
     def remote(src, dst, send, recv, device):
@@ -207,7 +212,7 @@
         )
         lane = lax.broadcasted_iota(jnp.int32, (Q * KO, LANES), 1)
         line = lax.broadcasted_iota(jnp.int32, (Q * KO, LANES), 0)
-        turns = turns + jnp.where(lane >= R, 8.0, 0.0) - jnp.where(line % 8 >= 4, 8.0, 0.0)
+        turns = turns + jnp.where(lane >= R, 8.0, 0.0) - jnp.where(line % SPAN >= EACH, 8.0, 0.0)
         turns = turns - G * jnp.floor(turns * (1.0 / G))
         high, low = split(jnp.cos(turns * (2.0 * math.pi / G)))
         rot[:, 0:128] = high
@@ -326,25 +331,25 @@
                 ))
             high, low = split(jnp.concatenate(cols, axis=1))
             value = dot(rot[...], jnp.concatenate([high, high], axis=0)) + dot(rot[:, 0:128], low)
-            for v in range(2):
-                for d in range(2 * Q):
-                    where = pl.ds(pl.multiple_of((STARTS[j] + 2 * u + v) * 8, 8), 8)
-                    phase_out[d % 2, d // 2, where, :] = value[
-                        d * 8 : (d + 1) * 8, v * LANES : (v + 1) * LANES
-                    ]
+            where = pl.ds(pl.multiple_of((STARTS[j] + 2 * u) * SPAN, 8), 2 * SPAN)
+            for d in range(GROUPS * Q):
+                lines = value[d * SPAN : (d + 1) * SPAN]
+                phase_out[d % GROUPS, d // GROUPS, where, :] = jnp.concatenate(
+                    [lines[:, 0:LANES], lines[:, LANES : 2 * LANES]], axis=0
+                )
             return carry
 
         lax.fori_loop(0, tiles // 2, step, 0)
-        mine = pl.ds(STARTS[j] * 8, tiles * 8)
-        there = pl.ds(pl.multiple_of((q * SHARE + STARTS[j]) * 8, 8), tiles * 8)
-        for g in range(2) if j == J - 1 else (slice(None),):
+        mine = pl.ds(STARTS[j] * SPAN, tiles * SPAN)
+        there = pl.ds(pl.multiple_of((q * SHARE + STARTS[j]) * SPAN, 8), tiles * SPAN)
+        for g in range(GROUPS) if j == J - 1 else (slice(None),):
             n = g if j == J - 1 else 0
             for i in range(1, Q):
                 p2a[j, n, i] = go(remote(
                     phase_out.at[g, qpeer(i), mine, :], phase_in.at[g, there, :],
                     sp.at[j, n, i], rp.at[j, n, i], (z * Q + qpeer(i), y),
                 ))
-        for g in range(2):
+        for g in range(GROUPS):
             phase_in[g, there, :] = phase_out[g, q, mine, :]
 
     steps = {
@@ -359,16 +364,16 @@
     lax.fori_loop(0, PAIRS, prepare_first, 0)
     second_copy.wait()
     lax.fori_loop(0, PAIRS, prepare_second, 0)
-    late = 2 * (Q - 1)
+    late = GROUPS * (Q - 1)
     for copy in copies1 + copies2 + waits[:-late]:
         copy.wait_send()
 
     def finish(k, carry):
-        g = k // 4
+        g = k // EACH
         planes = []
         for o in range(2):
             lines = both_parities(
-                [phase_in[g, pl.ds(8 * i + 4 * o + k % 4, B // 2, stride=24), :] for i in range(3)]
+                [phase_in[g, pl.ds(SPAN * i + EACH * o + k % EACH, B // 2, stride=3 * SPAN), :] for i in range(3)]
             )
             planes.append(split(jnp.concatenate(lines, axis=0)))
         (prh, prl), (pih, pil) = planes
@@ -398,11 +403,12 @@
     for j in range(J - 1):
         for i in range(1, Q):
             p2a[j, 0, i].wait_recv()
-    for g in range(2):
+    for g in range(GROUPS):
         for i in range(1, Q):
             p2a[J - 1, g, i].wait_recv()
-        lax.fori_loop(4 * g, 4 * g + 4, finish, 0)
-        outs.append(local(out_v.at[4 * g : 4 * g + 4], out_ref.at[4 * g : 4 * g + 4], out_sem.at[g]))
+        lax.fori_loop(EACH * g, EACH * (g + 1), finish, 0)
+        done = pl.ds(EACH * g, EACH)
+        outs.append(local(out_v.at[done], out_ref.at[done], out_sem.at[g]))
     for copy in waits[-late:]:
         copy.wait_send()
     for copy in outs:
@@ -451,17 +457,17 @@
             pltpu.VMEM((4, Q, 2 * SHARE, LANES), F32),
             pltpu.VMEM((Q, 2 * SHARE, LANES), F32),
             pltpu.VMEM((R * 2 * SHARE, LANES), F32),
-            pltpu.VMEM((2, Q, SHARE * 8, LANES), F32),
-            pltpu.VMEM((2, Q * SHARE * 8, LANES), F32),
+            pltpu.VMEM((GROUPS, Q, SHARE * SPAN, LANES), F32),
+            pltpu.VMEM((GROUPS, Q * SHARE * SPAN, LANES), F32),
             pltpu.VMEM((2, 256, LANES), F32),
             pltpu.VMEM((PAIRS, 2, 2, B, 256), BF16),
             pltpu.VMEM((PAIRS, 2, 2, 256, 256), BF16),
             pltpu.VMEM((PAIRS, TILES, LANES), F32),
-            dma((2,)), dma((6,)), dma((J, Q)), dma, dma,
+            dma((GROUPS,)), dma((6,)), dma((J, Q)), dma, dma,
             dma((Z,)), dma((Z,)), dma((Q,)), dma((Q,)),
             dma((J, 4)), dma((J, 4)),
             dma((J, Q)), dma((J, Q)), dma((J, 5, 2)), dma((J, 5, 2)),
-            dma((J, 2, Q)), dma((J, 2, Q)),
+            dma((J, GROUPS, Q)), dma((J, GROUPS, Q)),
         ],
         compiler_params=pltpu.CompilerParams(
             collective_id=0, has_side_effects=True, vmem_limit_bytes=60 * 2**20

time: 88.3 us -> 87.3 us (0.989)
  Pallas kernels: 84.5 us -> 83.5 us
    pallas_call x1, Pallas kernels: 84.5 us -> 83.5 us  [body(): pl.pallas_call(kernel, out_shape=jax.ShapeDtypeStruct((PAIRS, TILES, LANE...]
where the time goes in v4:
time: 87.3 us; the launch traced here: 87.2 us
  Pallas kernels  83.5 us (96%)
  local copies, waits for them, and re-layouts  2.37 us (3%)
  between operations  1.3 us (1%)
    pallas_call x1, Pallas kernels, body(): pl.pallas_call(kernel, out_shape=jax.ShapeDtypeStruct((PAIRS, TILES, LANE...  83.5 us
    unnamed x1, local copies, waits for them, and re-layouts  2.37 us

profile of v4, /device:TPU:1, one launch (start us, length us, event | category | flops | bytes accessed | tf_op | source)
XLA Modules:
  0.0 87.2 jit_solution(2608091408090486215)
XLA Ops:
  1.3 83.5 %shard_map.91 = f32[8,288,128]{2,1,0:T(8,128)} custom-call(f32[2,4,48]{2,1,0:T(4,128)} %bitcast.20, s32[1]{0:T(128)S(6)} %copy.14.owner_ref, s32[1]{0:T(128)S(6)} %copy.15.live_ref, s32[1,6]{1,0:T(1,128)} %triplets_ref.1, s32[3]{0:T(128)} %center_ref.1, s32[3,8]{1,0:T(4,128)} %bitcast.21, f32[48,36864]{1,0:T(8,128)} %bitcast.16, f32[8,576,128]{2,1,0:T(8,128)} %bitcast.18, ...), custom_call_target="tpu_custom_call" | custom-call | tf_op jit(solution)/shard_map/pallas_call | solution.py:436
  84.8 2.4 %copy.16 = f32[8,1,36864]{2,1,0:T(1,128)} copy(f32[8,1,36864]{2,1,0:T(1,128)} %bitcast.17) | data formatting | bytes 2359296

commit v5 on v4

--- a/solution.py
+++ b/solution.py
@@ -19,13 +19,12 @@
 PIECES = (8, 8, 8, 12)
 J = len(PIECES)
 ORDER = (
-    "C0", "Y0", "C1", "Y1", "C2", "Y2", "A0", "A1", "a0", "C3", "Y3", "A2",
-    "11", "12", "21", "b0", "A3", "22", "31", "13", "P0", "41", "32", "23",
-    "P1", "42", "33", "P2", "43", "P3",
+    "C0", "Y0", "C1", "Y1", "C2", "Y2", "A0", "A1", "10", "C3", "Y3", "A2",
+    "11", "20", "12", "21", "30", "A3", "22", "31", "40", "13", "P0", "41",
+    "32", "23", "P1", "42", "33", "P2", "43", "P3",
 )
 STARTS = tuple(sum(PIECES[:j]) for j in range(J))
 HALF = Q // 2
-FAST = 1
 PAIRS = 8
 KO = 2 * PAIRS
 GROUPS = 4
@@ -91,16 +90,6 @@
             (triplets_ref, triplets_s), (center_ref, center_s), (points_ref, points_v),
         ))
     ]
-    const_copies = {
-        (j, p): local(
-            const_ref.at[:, pl.ds((p * SHARE + STARTS[j]) * LANES, PIECES[j] * LANES)],
-            const_v.at[p, :, pl.ds(STARTS[j] * LANES, PIECES[j] * LANES)],
-            const_sem.at[j, p],
-        )
-        for j in range(J) for p in range(Q)
-    }
-    first_copy = local(first_ref, first_v, first_sem)
-    second_copy = local(second_ref, second_v, second_sem)
 
     tile[...] = jnp.zeros_like(tile)
     for copy in small:
@@ -141,6 +130,14 @@
         copy = remote(tile.at[0:16], got1.at[i], s1.at[i], r1.at[i], (zpeer(i) * Q + q, y))
         copy.start()
         copies1.append(copy)
+    const_copies = {
+        (j, p): local(
+            const_ref.at[:, pl.ds((p * SHARE + STARTS[j]) * LANES, PIECES[j] * LANES)],
+            const_v.at[p, :, pl.ds(STARTS[j] * LANES, PIECES[j] * LANES)],
+            const_sem.at[j, p],
+        )
+        for j in range(J) for p in range(Q)
+    }
 
     def paired(ref, k, start, stride):
         tiles = [ref[k, pl.ds(start + stride // 3 * i, B // 2, stride=stride), :] for i in range(3)]
@@ -217,6 +214,9 @@
         high, low = split(jnp.cos(turns * (2.0 * math.pi / G)))
         rot[:, 0:128] = high
         rot[:, 128:256] = low
+
+    first_copy = local(first_ref, first_v, first_sem)
+    second_copy = local(second_ref, second_v, second_sem)
 
     def contract(j):
         tiles = PIECES[j]
@@ -291,36 +291,10 @@
                 block, block, sz.at[j, i, side], rz.at[j, i, side], (((z + Z + sign) % Z) * Q + q, y)
             ))
 
-    def ring_send(j, n, side, origin, hops, half=None):
-        sign = 1 - 2 * side
-        base = ((z + Z - sign * origin) % Z) * Q
-        block = gathered.at[
-            slot_rows(j, base, Q) if half is None else slot_rows(j, base + HALF * half, HALF), :
-        ]
-        ring[j, n, side] = go(remote(
-            block, block, sz.at[j, n, side], rz.at[j, n, side], (((z + Z + sign * hops) % Z) * Q + q, y)
-        ))
-
-    def near_start(j):
-        for n in range(1, Q):
-            c2a[j, n].wait_recv()
-        for hops in (2, 1):
-            for side in range(2):
-                ring_send(j, hops, side, 0, hops)
-
-    def far_start(j):
-        for side in range(2):
-            ring[j, 2, side].wait_recv()
-        for side in range(2):
-            ring_send(j, 4, side, 2, 2, side)
-        for side in range(2):
-            ring_send(j, 3, side, 2, 1)
-
     def phase(j):
         tiles = PIECES[j]
-        for n in (1, 3, 4) if j < FAST else (4,):
-            for side in range(2):
-                ring[j, n, side].wait_recv()
+        for side in range(2):
+            ring[j, 4, side].wait_recv()
 
         def step(u, carry):
             cols = []
@@ -353,12 +327,12 @@
             phase_in[g, there, :] = phase_out[g, q, mine, :]
 
     steps = {
-        "C": contract, "Y": y_start, "A": c2a_start, "P": phase, "a": near_start, "b": far_start,
+        "C": contract, "Y": y_start, "A": c2a_start, "P": phase,
         **{str(i): functools.partial(ring_start, i=i) for i in range(1, 5)},
     }
     for name in ORDER:
         steps[name[0]](int(name[1]))
-        if name in ("a0", "10"):
+        if name == "10":
             rotation()
     first_copy.wait()
     lax.fori_loop(0, PAIRS, prepare_first, 0)

time: 87.3 us -> 86.7 us (level)
  no operation moved by 1% of the time
where the time goes in v5:
time: 86.7 us; the launch traced here: 86.5 us
  Pallas kernels  82.8 us (96%)
  local copies, waits for them, and re-layouts  2.37 us (3%)
  between operations  1.3 us (1%)
    pallas_call x1, Pallas kernels, body(): pl.pallas_call(kernel, out_shape=jax.ShapeDtypeStruct((PAIRS, TILES, LANE...  82.8 us
    unnamed x1, local copies, waits for them, and re-layouts  2.37 us

profile of v5, /device:TPU:1, one launch (start us, length us, event | category | flops | bytes accessed | tf_op | source)
XLA Modules:
  0.0 86.5 jit_solution(13645512261571270408)
XLA Ops:
  1.3 82.8 %shard_map.91 = f32[8,288,128]{2,1,0:T(8,128)} custom-call(f32[2,4,48]{2,1,0:T(4,128)} %bitcast.20, s32[1]{0:T(128)S(6)} %copy.14.owner_ref, s32[1]{0:T(128)S(6)} %copy.15.live_ref, s32[1,6]{1,0:T(1,128)} %triplets_ref.1, s32[3]{0:T(128)} %center_ref.1, s32[3,8]{1,0:T(4,128)} %bitcast.21, f32[48,36864]{1,0:T(8,128)} %bitcast.16, f32[8,576,128]{2,1,0:T(8,128)} %bitcast.18, ...), custom_call_target="tpu_custom_call" | custom-call | tf_op jit(solution)/shard_map/pallas_call | solution.py:410
  84.1 2.4 %copy.16 = f32[8,1,36864]{2,1,0:T(1,128)} copy(f32[8,1,36864]{2,1,0:T(1,128)} %bitcast.17) | data formatting | bytes 2359296
